TPU v7x, 128 devices: a whole 4x4x4 slice. The times are simulated.
128 devices in a mesh: row: 8 (over x_lo, y), col: 16 (over x_hi, z, core).
Axes of the slice: x: 4 (x_hi: 2, x_lo: 2; x = x_hi * 2 + x_lo), y: 4, z: 4, core: 2. Of those that a mesh axis runs over, the one named last changes fastest.
Arguments:
- features: bfloat16 [131072, 128], P(('row', 'col')), may hold values from -6 to 6
- weight: bfloat16 [128, 128], replicated, may hold values from -0.5 to 0.5
- cotangent: bfloat16 [131072, 128], P(('row', 'col')), may hold values from -6 to 6
- degree: int32 [131072], P(('row', 'col')), may hold values from 1 to 64
- tile_vals: bfloat16 [8192, 128, 128], P(('row', 'col')), may hold values from -0.25 to 0.25
- tile_rows: int32 [8192], P(('row', 'col')), may hold values from 0 to 7
- tile_cols: int32 [8192], P(('row', 'col')), may hold values from 0 to 7
- tile_live: int32 [8192], P(('row', 'col')), may hold values 0 or 1
- send_index: int32 [1024, 4], P(('row', 'col')), may hold values from 0 to 7
- remote_vals: bfloat16 [4096, 128, 128], P(('row', 'col')), may hold values from -0.5 to 0.5
- remote_rows: int32 [1024, 4], P(('row', 'col')), may hold values from 0 to 7
- remote_live: int32 [1024, 4], P(('row', 'col')), may hold values 0 or 1
Outputs:
- out_z: bfloat16 [131072, 128], P(('row', 'col'))
- grad_x: bfloat16 [131072, 128], P(('row', 'col'))
- grad_w: float32 [128, 128], replicated
Inputs may be any that keep to these rules, and one draw needn't show every extreme that they name: `tile_rows`: tile indices among one device's 1024 // 128 tiles.
All inputs are finite; a program needn't handle non-finite values. No bound on the sum of `tile_live` or of `remote_live` on one device may be relied on, other than what follows from the above.
Results may differ from a plain program's by a relative error of at most 0.0055.
Values may be sent and summed in bfloat16 or wider, within the bound.
A program may use at most 128 MiB of HBM per device.

v0:
```python
import jax
import jax.numpy as jnp
from jax import lax
from jax.sharding import PartitionSpec as P


def on_device(
    features,
    weight,
    cotangent,
    degree,
    tile_vals,
    tile_rows,
    tile_cols,
    tile_live,
    send_index,
    remote_vals,
    remote_rows,
    remote_live,
):
    highest = lax.Precision.HIGHEST
    node_count, feat_width = features.shape
    tile_size = tile_vals.shape[1]
    blocks = node_count // tile_size
    groups = lax.axis_size("col")
    per_piece = tile_vals.shape[0] // groups
    senders = send_index.shape[0]
    slot_count = send_index.shape[1]
    positions = jnp.arange(blocks, dtype=jnp.int32)
    inv_root = lax.rsqrt(degree.astype(jnp.float32))[:, None]
    scaled = (features.astype(jnp.float32) * inv_root).astype(jnp.bfloat16)
    scaled_tiles = scaled.reshape(blocks, tile_size, feat_width)
    dense_tiles = tile_vals.reshape(groups, per_piece, tile_size, tile_size)
    column_pick = (tile_cols.reshape(groups, per_piece)[:, :, None] == positions).astype(
        jnp.bfloat16
    )
    row_pick = (
        (tile_rows.reshape(groups, per_piece)[:, :, None] == positions)
        & (tile_live.reshape(groups, per_piece)[:, :, None] > 0)
    ).astype(jnp.bfloat16)
    sent_pick = (send_index[:, :, None] == positions).astype(jnp.bfloat16)
    remote_pick = ((remote_rows[:, :, None] == positions) & (remote_live[:, :, None] > 0)).astype(
        jnp.bfloat16
    )
    remote_tiles = remote_vals.reshape(senders, slot_count, tile_size, tile_size)
    outgoing = jnp.einsum(
        "rkb,bif->rkif", sent_pick, scaled_tiles, preferred_element_type=jnp.float32
    ).astype(jnp.bfloat16)
    arrived = lax.all_to_all(outgoing, "row", split_axis=0, concat_axis=0, tiled=True)
    remote_product = jnp.einsum(
        "rkij,rkjf->rkif", remote_tiles, arrived, preferred_element_type=jnp.float32
    )
    remote_sum = jnp.einsum(
        "rkb,rkif->bif", remote_pick.astype(jnp.float32), remote_product, precision=highest
    )
    shard_rows = lax.all_gather(scaled, "col", axis=0, tiled=True)
    pieces = shard_rows.shape[0] // node_count
    sub_tiles = dense_tiles
    sub_cols = column_pick
    sub_rows = row_pick
    shard_tiles = shard_rows.reshape(pieces, blocks, tile_size, feat_width)
    picked = jnp.einsum(
        "apb,abif->apif", sub_cols, shard_tiles, preferred_element_type=jnp.float32
    ).astype(jnp.bfloat16)
    product = jnp.einsum("apik,apkf->apif", sub_tiles, picked, preferred_element_type=jnp.float32)
    gathered = remote_sum + jnp.einsum(
        "apb,apif->bif", sub_rows.astype(jnp.float32), product, precision=highest
    )
    hidden = (inv_root * gathered.reshape(node_count, feat_width)).astype(jnp.bfloat16)
    out_z = jnp.dot(hidden, weight, preferred_element_type=jnp.float32).astype(jnp.bfloat16)
    weight_part = jnp.dot(hidden.T, cotangent, preferred_element_type=jnp.float32)
    grad_w = lax.psum(weight_part, ("row", "col"))
    back_grad = jnp.dot(cotangent, weight.T, preferred_element_type=jnp.float32)
    pulled = (inv_root * back_grad).astype(jnp.bfloat16)
    pulled_tiles = pulled.reshape(blocks, tile_size, feat_width)
    remote_chosen = jnp.einsum(
        "rkb,bif->rkif", remote_pick, pulled_tiles, preferred_element_type=jnp.float32
    ).astype(jnp.bfloat16)
    remote_back = jnp.einsum(
        "rkji,rkjf->rkif", remote_tiles, remote_chosen, preferred_element_type=jnp.float32
    )
    returned = lax.all_to_all(remote_back, "row", split_axis=0, concat_axis=0, tiled=True)
    remote_grad = jnp.einsum(
        "rkb,rkif->bif", sent_pick.astype(jnp.float32), returned, precision=highest
    ).reshape(node_count, feat_width)
    pieces = lax.axis_size("col") * node_count // node_count
    sub_tiles = dense_tiles
    sub_cols = column_pick
    sub_rows = row_pick
    chosen = jnp.einsum(
        "apb,bif->apif", sub_rows, pulled_tiles, preferred_element_type=jnp.float32
    ).astype(jnp.bfloat16)
    product = jnp.einsum("apki,apkf->apif", sub_tiles, chosen, preferred_element_type=jnp.float32)
    placed = jnp.einsum("apb,apif->abif", sub_cols.astype(jnp.float32), product, precision=highest)
    dense_grad = lax.psum_scatter(
        placed.reshape(pieces * node_count, feat_width), "col", scatter_dimension=0, tiled=True
    )
    grad_x = (inv_root * (dense_grad + remote_grad)).astype(jnp.bfloat16)
    return (out_z, grad_x, grad_w)


def solution(mesh):
    placed = (
        P(("row", "col"), None),
        P(),
        P(("row", "col"), None),
        P(("row", "col")),
        P(("row", "col"), None, None),
        P(("row", "col")),
        P(("row", "col")),
        P(("row", "col")),
        P(("row", "col"), None),
        P(("row", "col"), None, None),
        P(("row", "col"), None),
        P(("row", "col"), None),
    )
    return jax.shard_map(
        on_device,
        mesh=mesh,
        in_specs=placed,
        out_specs=(P(("row", "col"), None), P(("row", "col"), None), P()),
        check_vma=False,
    )
```

profile of v0, /device:TPU:1, one launch (start us, length us, event | category | flops | bytes accessed | tf_op | source)
XLA Modules:
  0.0 333.7 jit_solution(4638667078796812974)
XLA Ops:
  8.1 1.9 multiply_convert_fusion
  13.6 3.2 convolution_bitcast_fusion
  16.9 5.3 %copy.77 = f32[16,4,128,128]{3,1,2,0:T(4,128)} copy(f32[16,4,128,128]{2,3,1,0:T(8,128)} %convolution_bitcast_fusion) | data formatting | bytes 8388608 | tf_op jit(solution)/shard_map/apki,apkf->apif/dot_general | solution.py:93
  22.3 7.0 %fusion.25 = f32[16,8,128,128]{3,1,2,0:T(8,128)S(1)} fusion(f32[16,4,128,128]{3,1,2,0:T(4,128)} %copy.77, s32[16,4]{1,0:T(8,128)S(1)} %eq.66), kind=kOutput, calls=%fused_computation.36 | convolution fusion | flops 100663808 | bytes 12583168 | tf_op jit(solution)/shard_map/apb,apif->abif/dot_general | solution.py:94
  29.3 4.7 %copy.78 = f32[16,8,128,128]{3,2,1,0:T(8,128)} copy(f32[16,8,128,128]{3,1,2,0:T(8,128)S(1)} %fusion.25) | data formatting | bytes 16777216 | tf_op jit(solution)/shard_map/apb,apif->abif/dot_general | solution.py:94
  35.5 1.2 copy.65
  36.7 6.0 %all-to-all-start = ((bf16[8,4,128,128]{3,2,1,0:T(8,128)(2,1)}), bf16[8,4,128,128]{3,2,1,0:T(8,128)(2,1)S(1)}, u32[]{:S(2)}, u32[]{:S(2)}) async-start(bf16[8,4,128,128]{3,2,1,0:T(8,128)(2,1)} %copy.65), calls=%async_computation | async-start | bytes 2097152 | tf_op jit(solution)/shard_map/all_to_all | solution.py:49
  43.2 3.1 convolution_bitcast_fusion.2
  46.3 3.1 copy.81
  49.3 12.9 %all-to-all-done = bf16[8,4,128,128]{3,2,1,0:T(8,128)(2,1)S(1)} async-done(((bf16[8,4,128,128]{3,2,1,0:T(8,128)(2,1)}), bf16[8,4,128,128]{3,2,1,0:T(8,128)(2,1)S(1)}, u32[]{:S(2)}, u32[]{:S(2)}) %all-to-all-start) | async-done | bytes 1048608 | tf_op jit(solution)/shard_map/all_to_all | solution.py:49
  62.3 4.4 %all-to-all-start.1 = ((f32[8,4,128,128]{3,1,2,0:T(4,128)}), f32[8,4,128,128]{3,1,2,0:T(4,128)}, u32[]{:S(2)}, u32[]{:S(2)}) async-start(f32[8,4,128,128]{3,1,2,0:T(4,128)} %copy.81), calls=%async_computation.2 | async-start | bytes 4194304 | tf_op jit(solution)/shard_map/all_to_all | solution.py:82
  66.9 3.4 %convolution_bitcast_fusion.3 = f32[8,4,128,128]{2,3,1,0:T(8,128)} fusion(bf16[8,4,128,128]{3,2,1,0:T(8,128)(2,1)S(1)} %all-to-all-done, bf16[8,4,128,128]{3,2,1,0:T(8,128)(2,1)} %bitcast.92), kind=kOutput, calls=%fused_computation.11 | convolution fusion | flops 134217728 | bytes 4194304 | tf_op jit(solution)/shard_map/rkij,rkjf->rkif/dot_general | solution.py:50
  70.3 3.1 copy.68
  73.5 18.3 %all-to-all-done.1 = f32[8,4,128,128]{3,1,2,0:T(4,128)} async-done(((f32[8,4,128,128]{3,1,2,0:T(4,128)}), f32[8,4,128,128]{3,1,2,0:T(4,128)}, u32[]{:S(2)}, u32[]{:S(2)}) %all-to-all-start.1) | async-done | bytes 2097184 | tf_op jit(solution)/shard_map/all_to_all | solution.py:82
  91.8 4.6 %fusion.9 = f32[8,128,128]{2,0,1:T(8,128)S(1)} fusion(f32[8,4,128,128]{3,1,2,0:T(4,128)} %all-to-all-done.1, s32[8,4]{0,1:T(4,128)S(1)} %copy-done.5), kind=kOutput, calls=%fused_computation.14 | convolution fusion | flops 50331904 | bytes 2621568 | tf_op jit(solution)/shard_map/rkb,rkif->bif/dot_general | solution.py:83
  96.5 5.4 %fusion.6 = bf16[16,4,128,128]{3,1,2,0:T(4,128)(2,1)S(1)} fusion(bf16[16,8,128,128]{3,2,1,0:T(8,128)(2,1)} %bitcast.90, s32[16,4]{1,0:T(8,128)S(1)} %eq.66), kind=kOutput, calls=%fused_computation.8 | convolution fusion | flops 17826304 | bytes 6291712 | tf_op jit(solution)/shard_map/apb,abif->apif/dot_general | solution.py:62
  101.9 3.6 %convolution_bitcast_fusion.1 = f32[16,4,128,128]{2,3,1,0:T(8,128)} fusion(bf16[16,4,128,128]{3,2,1,0:T(8,128)(2,1)S(1)} %bitcast.87, bf16[16,4,128,128]{3,1,2,0:T(4,128)(2,1)S(1)} %fusion.6), kind=kOutput, calls=%fused_computation.3 | convolution fusion | flops 268435456 | bytes 8388608 | tf_op jit(solution)/shard_map/apik,apkf->apif/dot_general | solution.py:65
  105.5 5.6 %copy.73 = f32[16,4,128,128]{3,0,1,2:T(8,128)} copy(f32[16,4,128,128]{2,3,1,0:T(8,128)} %convolution_bitcast_fusion.1) | data formatting | bytes 8388608 | tf_op jit(solution)/shard_map/apik,apkf->apif/dot_general | solution.py:65
  111.1 4.5 %convolution_bitcast_fusion.4 = f32[8,128,128]{2,0,1:T(8,128)S(1)} fusion(f32[16,4,128,128]{3,0,1,2:T(8,128)} %copy.73, s32[16,4]{0,1:T(4,128)S(1)} %copy.69, pred[16,4]{0,1:T(4,128)(4,1)S(1)} %copy.70), kind=kOutput, calls=%fused_computation.15 | convolution fusion | flops 100664320 | bytes 4718912 | tf_op jit(solution)/shard_map/apb,apif->bif/dot_general | solution.py:66
  116.6 66.2 %reduce-scatter.2.cloned.1.call-done = f32[1024,128]{1,0:T(8,128)} async-done(((f32[16384,128]{1,0:T(8,128)}), f32[1024,128]{1,0:T(8,128)}) %reduce-scatter.2.cloned.1.call-update) | async-done | bytes 524304 | tf_op jit(solution)/shard_map/reduce_scatter | solution.py:95
  182.8 1.9 fusion.16
  184.7 1.8 fusion.54
  187.5 138.2 %all-reduce.2.cloned.1.call-done = f32[128,128]{1,0:T(8,128)} async-done(((f32[128,128]{1,0:T(8,128)}), f32[128,128]{1,0:T(8,128)}) %all-reduce.2.cloned.1.call-update) | async-done | bytes 65552 | tf_op jit(solution)/shard_map/psum | solution.py:72
  325.7 1.5 copy.123
  (39 shorter events, 8.8 us)
Async XLA Ops:
  7.2 6.5 %copy-start = (bf16[64,128,128]{2,1,0:T(8,128)(2,1)S(1)}, bf16[64,128,128]{2,1,0:T(8,128)(2,1)}, u32[]{:S(2)}) copy-start(bf16[64,128,128]{2,1,0:T(8,128)(2,1)} %param.16) | copy-start | bytes 6291460
  7.2 89.3 %all-gather.2.cloned.1.call-start = ((), (), s32[]{:S(2)}) async-start(), calls=%async_computation.3 | async-start | bytes 4456448 | tf_op jit(solution)/shard_map/all_gather | solution.py:56
  9.9 172.8 %reduce-scatter.2.cloned.1.call-start = ((), (), s32[]{:S(2)}) async-start(), calls=%async_computation.4 | async-start | bytes 8912896 | tf_op jit(solution)/shard_map/reduce_scatter | solution.py:95
  16.9 5.3 %copy-start.7 = (s32[64]{0:T(128)S(1)}, s32[64]{0:T(128)}, u32[]{:S(2)}) copy-start(s32[64]{0:T(128)} %param.18) | copy-start | bytes 772
  34.0 0.9 copy-start.2
  34.0 1.0 copy-start.5
  35.4 7.2 %copy-start.6 = (s32[8,4]{0,1:T(4,128)S(1)}, s32[8,4]{0,1:T(4,128)}, u32[]{:S(2)}) copy-start(s32[8,4]{0,1:T(4,128)} %param.23) | copy-start | bytes 388
  35.5 7.3 %copy-start.4 = (s32[8,4]{0,1:T(4,128)S(1)}, s32[8,4]{0,1:T(4,128)}, u32[]{:S(2)}) copy-start(s32[8,4]{0,1:T(4,128)} %param.22) | copy-start | bytes 388
  36.7 25.6 %all-to-all-start = ((bf16[8,4,128,128]{3,2,1,0:T(8,128)(2,1)}), bf16[8,4,128,128]{3,2,1,0:T(8,128)(2,1)S(1)}, u32[]{:S(2)}, u32[]{:S(2)}) async-start(bf16[8,4,128,128]{3,2,1,0:T(8,128)(2,1)} %copy.65), calls=%async_computation | async-start | bytes 2097152 | tf_op jit(solution)/shard_map/all_to_all | solution.py:49
  62.3 29.5 %all-to-all-start.1 = ((f32[8,4,128,128]{3,1,2,0:T(4,128)}), f32[8,4,128,128]{3,1,2,0:T(4,128)}, u32[]{:S(2)}, u32[]{:S(2)}) async-start(f32[8,4,128,128]{3,1,2,0:T(4,128)} %copy.81), calls=%async_computation.2 | async-start | bytes 4194304 | tf_op jit(solution)/shard_map/all_to_all | solution.py:82
  66.7 259.0 %all-reduce.2.cloned.1.call-start = ((), (), s32[]{:S(2)}) async-start(), calls=%async_computation.5 | async-start | bytes 131072 | tf_op jit(solution)/shard_map/psum | solution.py:72
  111.1 4.5 %copy-start.1 = (f32[8,4,128,128]{3,0,1,2:T(8,128)S(1)}, f32[8,4,128,128]{3,0,1,2:T(8,128)}, u32[]{:S(2)}) copy-start(f32[8,4,128,128]{3,0,1,2:T(8,128)} %copy.68) | copy-start | bytes 6291460
  116.4 70.1 %copy-start.3 = (bf16[128,128]{1,0:T(8,128)(2,1)S(1)}, bf16[128,128]{1,0:T(8,128)(2,1)}, u32[]{:S(2)}) copy-start(bf16[128,128]{1,0:T(8,128)(2,1)} %param.13) | copy-start | bytes 98308
Sparse Core Ops, SparseCore 0:
  11.1 68.0 all-gather.1
  83.4 99.2 reduce-scatter.1
  188.1 137.5 all-reduce.1
where the time goes:
time: 335 us; the launch traced here: 334 us
  waiting for transfers between devices  236 us (70%)
  matrix products  41.4 us (12%)
  local copies, waits for them, and re-layouts  26.7 us (8%)
  between operations  13.9 us (4%)
  starting transfers between devices  10.7 us (3%)
  other arithmetic  5.31 us (2%)
    psum x1, waiting for transfers between devices, on_device(): grad_w = lax.psum(weight_part, ('row', 'col'))  138 us
    reduce_scatter x1, waiting for transfers between devices, on_device(): lax.psum_scatter(placed.reshape(pieces * node_count, feat_width), 'col',...  66.2 us
    all_to_all x1, waiting for transfers between devices, on_device(): lax.all_to_all(remote_back, 'row', split_axis=0, concat_axis=0, tiled=True)  18.3 us
    all_to_all x1, waiting for transfers between devices, on_device(): lax.all_to_all(outgoing, 'row', split_axis=0, concat_axis=0, tiled=True)  12.9 us
    dot_general x1, matrix products, on_device(): jnp.einsum('apb,apif->abif', sub_cols.astype(jnp.float32), product, preci...  7.03 us
  transfers between devices with their start and end apart: 5, of which 4 were waited for; matrix products, arithmetic and copies ran while one was open for 19% of the time, Pallas kernels for 0%

commit v1 on v0

v1 whole, which is shorter than its diff:
```python
import jax
import jax.numpy as jnp
from jax import lax
from jax.experimental import pallas as pl
from jax.experimental.pallas import tpu as pltpu
from jax.sharding import PartitionSpec as P

MESH = pl.DeviceIdType.MESH
BF16 = jnp.bfloat16
F32 = jnp.float32
TILE = 128
BLOCKS = 8
SLOTS = 4
HALF = 4
ROW_RELS = [(a, b) for a in range(2) for b in range(4)]
COL_RELS = [(a, b) for a in range(2) for b in range(4)]


def spot():
    row, col = lax.axis_index("row"), lax.axis_index("col")
    return row // 4, row % 4, col // 8, (col // 2) % 4, col % 2


def row_of(rel):
    x_lo, y, _, _, _ = spot()
    return ((x_lo + rel[0]) % 2) * 4 + (y + rel[1]) % 4


def col_of(rel, flip=0):
    _, _, x_hi, z, core = spot()
    return ((x_hi + rel[0]) % 2) * 8 + ((z + rel[1]) % 4) * 2 + (core + flip) % 2


def back_rel(rel):
    return (-rel[0]) % 2, (-rel[1]) % 4


def kernel(
    features,
    weight,
    cotangent,
    degree,
    tile_rows,
    tile_cols,
    tile_live,
    send_index,
    remote_rows,
    remote_live,
    tile_hbm,
    remote_hbm,
    out_z,
    grad_x,
    grad_w,
    tiles,
    remotes,
    inv_col,
    pulled,
    cot_t,
    prod,
    gathered,
    spread,
    outgoing,
    arrived,
    sent_back,
    returned,
    cross_out,
    cross_in,
    sums,
    ring_half,
    ring_full,
    pair_out,
    pair_in,
    wg,
    wg_core,
    wg_part,
    wg_col,
    wg_mine,
    wg_row,
    wg_half,
    wg_other,
    wg_all,
    send_sem,
    recv_sem,
    local_sem,
    *blocks,
):
    row, col = lax.axis_index("row"), lax.axis_index("col")
    _, _, x_hi, z, core = spot()
    copies = []

    def remote(src, dst, target):
        i = len(copies)
        copy = pltpu.make_async_remote_copy(
            src_ref=src,
            dst_ref=dst,
            send_sem=send_sem.at[i],
            recv_sem=recv_sem.at[i],
            device_id=target,
            device_id_type=MESH,
        )
        copies.append(copy)
        copy.start()
        return copy

    def to_row(rel):
        return (row_of(rel), col)

    def to_col(rel, flip=0):
        return (row, col_of(rel, flip))

    load_tiles = pltpu.make_async_copy(tile_hbm, tiles, local_sem.at[0])
    load_remotes = pltpu.make_async_copy(remote_hbm, remotes, local_sem.at[1])
    load_tiles.start()
    load_remotes.start()

    barrier = pltpu.get_barrier_semaphore()
    peers = [to_row(rel) for rel in ROW_RELS[1:]]
    peers += [to_col(rel) for rel in COL_RELS[1:]]
    peers += [to_col((0, 0), 1)]
    for peer in peers:
        pl.semaphore_signal(barrier, inc=1, device_id=peer, device_id_type=MESH)

    def block(rel, flip=0):
        return blocks[(rel[0] * 4 + rel[1] % 4) * 2 + flip]

    own = block((0, 0))
    inv_row = lax.rsqrt(degree[...].astype(F32))
    for b in range(BLOCKS):
        at = pl.ds(b * TILE, TILE)
        across = jnp.broadcast_to(inv_row[b : b + 1, :], (TILE, TILE)).T
        inv_col[at, :] = across
        own[b] = (features[at, :].astype(F32) * across).astype(BF16)

    pl.semaphore_wait(barrier, len(peers))

    def rows(ref, lo, hi):
        return ref.at[pl.ds(lo, hi - lo)]

    def push(rel_src, rel_dst, target, lo, hi):
        return remote(rows(block(rel_src), lo, hi), rows(block(rel_dst), lo, hi), target)

    z_up, z_down, x_far = to_col((0, 1)), to_col((0, 3)), to_col((1, 0))
    up_a = push((0, 0), (0, 3), z_up, 0, HALF)
    down_a = push((0, 0), (0, 1), z_down, HALF, BLOCKS)
    far_a = push((0, 0), (1, 0), x_far, 0, HALF)
    far_b = push((0, 0), (1, 0), x_far, HALF, BLOCKS)
    up_b = push((0, 0), (0, 3), z_up, HALF, BLOCKS)
    down_b = push((0, 0), (0, 1), z_down, 0, HALF)

    def share(rel):
        return remote(block(rel), block(rel, 1), to_col((0, 0), 1))

    shared = {(0, 0): share((0, 0))}

    row_sent = {}
    for i, rel in enumerate(ROW_RELS):
        owner = row_of(rel)
        for k in range(SLOTS):
            tile = send_index[owner, k]
            outgoing[i * SLOTS + k] = own[tile]
        if i:
            there = ROW_RELS.index(back_rel(rel))
            row_sent[back_rel(rel)] = remote(
                outgoing.at[pl.ds(i * SLOTS, SLOTS)],
                arrived.at[pl.ds(there * SLOTS, SLOTS)],
                to_row(rel),
            )

    for b in range(BLOCKS):
        at = pl.ds(b * TILE, TILE)
        back = lax.dot_general(
            weight[...], cotangent[at, :], (((1,), (1,)), ((), ())), preferred_element_type=F32
        )
        pulled[b] = (back * inv_row[b : b + 1, :]).astype(BF16)
        cot_t[:, at] = cotangent[at, :].T

    def mask(hit, live):
        return (hit.astype(jnp.int32) * live).astype(F32)

    def spread_out(marks, lives, store, extra=None):
        def body(b, carry):
            value = mask(marks[0] == b, lives[0]) * prod[0]
            for j in range(1, SLOTS):
                value += mask(marks[j] == b, lives[j]) * prod[j]
            store(b, value)
            return carry

        lax.fori_loop(0, BLOCKS, body, 0)

    def add_to(ref, first=False):
        def store(b, value):
            ref[b] = value if first else ref[b] + value

        return store

    def dense_back(rel, flip):
        base = col_of(rel, flip) * SLOTS
        for j in range(SLOTS):
            prod[j] = jnp.dot(
                pulled[tile_rows[base + j]], tiles[base + j], preferred_element_type=F32
            )
        marks = [tile_cols[base + j] for j in range(SLOTS)]
        lives = [tile_live[base + j] for j in range(SLOTS)]
        return marks, lives

    def place(rel):
        return rel[0] * 4 + rel[1] % 4

    crossed = {}

    def back_cross(rel):
        at = place(rel)

        def store(b, value):
            cross_out[at, b] = value.astype(BF16)

        spread_out(*dense_back(rel, 1), store)
        crossed[rel] = remote(cross_out.at[at], cross_in.at[at], to_col((0, 0), 1))

    def back_own(rel):
        at = place(rel)
        crossed[rel].wait_recv()

        def store(b, value):
            value += cross_in[at, b].astype(F32)
            if rel == (0, 0):
                spread[b] = value
            else:
                sums[at, b] = value.astype(BF16)

        spread_out(*dense_back(rel, 0), store)

    def forward(rel, flip, first=False):
        base = col_of(rel, flip) * SLOTS
        source = block(rel, flip)
        for j in range(SLOTS):
            prod[j] = jnp.dot(
                tiles[base + j], source[tile_cols[base + j]], preferred_element_type=F32
            )
        marks = [tile_rows[base + j] for j in range(SLOTS)]
        lives = [tile_live[base + j] for j in range(SLOTS)]
        spread_out(marks, lives, add_to(gathered, first))

    def remote_forward(i):
        rel = ROW_RELS[i]
        owner = row_of(rel)
        if i:
            row_sent[rel].wait_recv()
        source = arrived if i else outgoing
        for k in range(SLOTS):
            prod[k] = jnp.dot(
                remotes[owner * SLOTS + k], source[i * SLOTS + k], preferred_element_type=F32
            )
        marks = [remote_rows[owner, k] for k in range(SLOTS)]
        lives = [remote_live[owner, k] for k in range(SLOTS)]
        spread_out(marks, lives, add_to(gathered))

    back_sent = {}

    def remote_back(i):
        rel = ROW_RELS[i]
        owner = row_of(rel)
        for k in range(SLOTS):
            value = jnp.dot(
                pulled[remote_rows[owner, k]],
                remotes[owner * SLOTS + k],
                preferred_element_type=F32,
            )
            live = remote_live[owner, k].astype(F32)
            sent_back[i * SLOTS + k] = (value * live).astype(BF16)
        if i:
            there = ROW_RELS.index(back_rel(rel))
            back_sent[back_rel(rel)] = remote(
                sent_back.at[pl.ds(i * SLOTS, SLOTS)],
                returned.at[pl.ds(there * SLOTS, SLOTS)],
                to_row(rel),
            )

    def remote_return(i):
        rel = ROW_RELS[i]
        owner = row_of(rel)
        if i:
            back_sent[rel].wait_recv()
        source = returned if i else sent_back
        for k in range(SLOTS):
            prod[k] = source[i * SLOTS + k].astype(F32)
        marks = [send_index[owner, k] for k in range(SLOTS)]
        spread_out(marks, [jnp.int32(1)] * SLOTS, add_to(spread))

    load_tiles.wait()
    back_cross((1, 2))
    back_cross((1, 1))
    up_a.wait_recv()
    up_c = push((0, 3), (0, 2), z_up, 0, HALF)
    down_a.wait_recv()
    down_c = push((0, 1), (0, 2), z_down, HALF, BLOCKS)
    far_a.wait_recv()
    far_up_a = push((1, 0), (1, 3), z_up, 0, HALF)
    back_cross((1, 3))
    far_b.wait_recv()
    far_down_a = push((1, 0), (1, 1), z_down, HALF, BLOCKS)
    far_up_b = push((1, 0), (1, 3), z_up, HALF, BLOCKS)
    far_down_b = push((1, 0), (1, 1), z_down, 0, HALF)
    shared[1, 0] = share((1, 0))
    up_b.wait_recv()
    shared[0, 3] = share((0, 3))
    down_b.wait_recv()
    shared[0, 1] = share((0, 1))
    load_remotes.wait()
    for i in range(1, len(ROW_RELS)):
        remote_back(i)
    back_cross((1, 0))
    for rel in [(0, 2), (0, 1), (0, 3), (0, 0)]:
        back_cross(rel)
    far_up_a.wait_recv()
    far_up_c = push((1, 3), (1, 2), z_up, 0, HALF)
    far_down_a.wait_recv()
    far_down_c = push((1, 1), (1, 2), z_down, HALF, BLOCKS)
    up_c.wait_recv()
    down_c.wait_recv()
    shared[0, 2] = share((0, 2))
    back_own((1, 2))

    ring = {}

    def ring_start(a):
        ring["up_half", a] = remote(
            sums.at[place((a, 2)), pl.ds(0, HALF)], ring_half.at[a, pl.ds(0, HALF)], z_up
        )
        ring["down_half", a] = remote(
            sums.at[place((a, 2)), pl.ds(HALF, HALF)], ring_half.at[a, pl.ds(HALF, HALF)], z_down
        )

    def ring_early(a):
        ring["up_early", a] = remote(
            sums.at[place((a, 1)), pl.ds(HALF, HALF)], ring_full.at[a, 0, pl.ds(HALF, HALF)], z_up
        )
        ring["down_early", a] = remote(
            sums.at[place((a, 3)), pl.ds(0, HALF)], ring_full.at[a, 1, pl.ds(0, HALF)], z_down
        )

    def ring_late(a):
        for name, rel, lo, side, target in (
            ("up", (a, 1), 0, 0, z_up),
            ("down", (a, 3), HALF, 1, z_down),
        ):
            ring[name + "_half", a].wait_recv()
            at = place(rel)

            def body(b, carry):
                total = sums[at, b].astype(F32) + ring_half[a, b].astype(F32)
                sums[at, b] = total.astype(BF16)
                return carry

            lax.fori_loop(lo, lo + HALF, body, 0)
            ring[name + "_late", a] = remote(
                sums.at[at, pl.ds(lo, HALF)], ring_full.at[a, side, pl.ds(lo, HALF)], target
            )

    ring_start(1)
    back_own((1, 1))
    back_own((1, 3))
    ring_early(1)
    back_own((0, 2))
    ring_start(0)
    back_own((0, 1))
    back_own((0, 3))
    ring_early(0)
    back_own((1, 0))
    back_own((0, 0))

    forward((0, 0), 0, True)
    shared[0, 0].wait_recv()
    forward((0, 0), 1)
    for i in range(len(ROW_RELS)):
        remote_forward(i)
    ring_late(1)
    forward((1, 0), 0)
    forward((0, 1), 0)
    forward((0, 3), 0)
    forward((0, 2), 0)
    for rel in [(1, 0), (0, 1), (0, 3), (0, 2)]:
        shared[rel].wait_recv()
        forward(rel, 1)
    far_up_b.wait_recv()
    shared[1, 3] = share((1, 3))
    far_down_b.wait_recv()
    shared[1, 1] = share((1, 1))
    far_up_c.wait_recv()
    far_down_c.wait_recv()
    shared[1, 2] = share((1, 2))
    ring_late(0)
    for rel in [(1, 3), (1, 1), (1, 2)]:
        forward(rel, 0)
    for rel in [(1, 3), (1, 1), (1, 2)]:
        shared[rel].wait_recv()
        forward(rel, 1)

    total = jnp.zeros((TILE, TILE), F32)
    for b in range(BLOCKS):
        at = pl.ds(b * TILE, TILE)
        hidden = (inv_col[at, :] * gathered[b]).astype(BF16)
        total += jnp.dot(cot_t[:, at], hidden, preferred_element_type=F32)
        out_z[at, :] = jnp.dot(hidden, weight[...], preferred_element_type=F32).astype(BF16)
    wg[...] = total
    half = TILE // 2
    part = half // 8
    mine_half = pl.ds(pl.multiple_of(core * half, half), half)
    other_half = pl.ds(pl.multiple_of((1 - core) * half, half), half)
    halves = remote(wg.at[other_half], wg_core, to_col((0, 0), 1))
    halves.wait_recv()
    wg_part[...] = wg[mine_half, :] + wg_core[...]
    here = x_hi * 4 + z

    def chunk(at):
        return pl.ds(pl.multiple_of(at * part, part), part)

    col_parts = []
    for rel in COL_RELS[1:]:
        there = col_of(rel) // 2
        col_parts.append(remote(wg_part.at[chunk(there)], wg_col.at[here], to_col(rel)))
    wg_col[here] = wg_part[chunk(here), :]

    def pair_send():
        for name in ("up_early", "down_early", "up_late", "down_late"):
            ring[name, 1].wait_recv()
        at = place((1, 0))

        def body(b, carry):
            value = sums[at, b].astype(F32)
            value += ring_full[1, 0, b].astype(F32) + ring_full[1, 1, b].astype(F32)
            pair_out[b] = value.astype(BF16)
            return carry

        lax.fori_loop(0, BLOCKS, body, 0)
        return remote(pair_out, pair_in, x_far)

    for copy in col_parts:
        copy.wait_recv()
    wg_mine[...] = jnp.sum(wg_col[...], axis=0)
    row_parts = []
    for rel in ROW_RELS[1:]:
        row_parts.append(remote(wg_mine, wg_row.at[row], to_row(rel)))
    wg_row[row] = wg_mine[...]
    for i in range(len(ROW_RELS)):
        if i == 0:
            remote_back(0)
        remote_return(i)
    for copy in row_parts:
        copy.wait_recv()
    wg_half[here] = jnp.sum(wg_row[...], axis=0)
    col_full = []
    for rel in COL_RELS[1:]:
        col_full.append(remote(wg_half.at[here], wg_half.at[here], to_col(rel)))
    pair = pair_send()
    for copy in col_full:
        copy.wait_recv()
    full = remote(wg_half, wg_other, to_col((0, 0), 1))
    wg_all[mine_half, :] = wg_half[...].reshape(half, TILE)
    full.wait_recv()
    wg_all[other_half, :] = wg_other[...].reshape(half, TILE)
    grad_w[...] = wg_all[...].T

    for name in ("up_early", "down_early", "up_late", "down_late"):
        ring[name, 0].wait_recv()
    pair.wait_recv()
    for b in range(BLOCKS):
        value = spread[b] + pair_in[b].astype(F32)
        value += ring_full[0, 0, b].astype(F32) + ring_full[0, 1, b].astype(F32)
        value *= inv_row[b : b + 1, :]
        grad_x[pl.ds(b * TILE, TILE), :] = value.T.astype(BF16)
    for copy in copies:
        copy.wait_send()


def on_device(
    features,
    weight,
    cotangent,
    degree,
    tile_vals,
    tile_rows,
    tile_cols,
    tile_live,
    send_index,
    remote_vals,
    remote_rows,
    remote_live,
):
    nodes, width = features.shape
    vmem = pl.BlockSpec(memory_space=pltpu.VMEM)
    smem = pl.BlockSpec(memory_space=pltpu.SMEM)
    hbm = pl.BlockSpec(memory_space=pl.ANY)
    stack = (BLOCKS, TILE, TILE)
    n_copies = 96
    return pl.pallas_call(
        kernel,
        out_shape=(
            jax.ShapeDtypeStruct((nodes, width), BF16),
            jax.ShapeDtypeStruct((nodes, width), BF16),
            jax.ShapeDtypeStruct((TILE, TILE), F32),
        ),
        in_specs=[vmem] * 4 + [smem] * 6 + [hbm] * 2,
        out_specs=(vmem, vmem, vmem),
        scratch_shapes=[
            pltpu.VMEM(tile_vals.shape, BF16),
            pltpu.VMEM(remote_vals.shape, BF16),
            pltpu.VMEM((nodes, TILE), F32),
            pltpu.VMEM(stack, BF16),
            pltpu.VMEM((TILE, nodes), BF16),
            pltpu.VMEM((SLOTS, TILE, TILE), F32),
            pltpu.VMEM(stack, F32),
            pltpu.VMEM(stack, F32),
            pltpu.VMEM((32, TILE, TILE), BF16),
            pltpu.VMEM((32, TILE, TILE), BF16),
            pltpu.VMEM((32, TILE, TILE), BF16),
            pltpu.VMEM((32, TILE, TILE), BF16),
            pltpu.VMEM((8,) + stack, BF16),
            pltpu.VMEM((8,) + stack, BF16),
            pltpu.VMEM((8,) + stack, BF16),
            pltpu.VMEM((2,) + stack, BF16),
            pltpu.VMEM((2, 2) + stack, BF16),
            pltpu.VMEM(stack, BF16),
            pltpu.VMEM(stack, BF16),
            pltpu.VMEM((TILE, TILE), F32),
            pltpu.VMEM((TILE // 2, TILE), F32),
            pltpu.VMEM((TILE // 2, TILE), F32),
            pltpu.VMEM((8, 8, TILE), F32),
            pltpu.VMEM((8, TILE), F32),
            pltpu.VMEM((8, 8, TILE), F32),
            pltpu.VMEM((8, 8, TILE), F32),
            pltpu.VMEM((8, 8, TILE), F32),
            pltpu.VMEM((TILE, TILE), F32),
            pltpu.SemaphoreType.DMA((n_copies,)),
            pltpu.SemaphoreType.DMA((n_copies,)),
            pltpu.SemaphoreType.DMA((2,)),
        ]
        + [pltpu.VMEM(stack, BF16)] * 16,
        compiler_params=pltpu.CompilerParams(
            collective_id=0, has_side_effects=True, vmem_limit_bytes=48 * 2**20
        ),
    )(
        features,
        weight,
        cotangent,
        degree.reshape(BLOCKS, TILE),
        tile_rows,
        tile_cols,
        tile_live,
        send_index,
        remote_rows,
        remote_live,
        tile_vals,
        remote_vals,
    )


def solution(mesh):
    placed = (
        P(("row", "col"), None),
        P(),
        P(("row", "col"), None),
        P(("row", "col")),
        P(("row", "col"), None, None),
        P(("row", "col")),
        P(("row", "col")),
        P(("row", "col")),
        P(("row", "col"), None),
        P(("row", "col"), None, None),
        P(("row", "col"), None),
        P(("row", "col"), None),
    )
    return jax.shard_map(
        on_device,
        mesh=mesh,
        in_specs=placed,
        out_specs=(P(("row", "col"), None), P(("row", "col"), None), P()),
        check_vma=False,
    )
```

time: 335 us -> 72.9 us (0.22)
  waiting for transfers between devices: 236 us -> 0 us
  Pallas kernels: 0 us -> 59.1 us
  matrix products: 41.4 us -> 0 us
  local copies, waits for them, and re-layouts: 26.7 us -> 12.4 us
  between operations: 13.9 us -> 0.65 us
  starting transfers between devices: 10.7 us -> 0 us
  other arithmetic: 5.31 us -> 0 us
    psum x1 -> x0, waiting for transfers between devices: 138 us -> none  [on_device(): grad_w = lax.psum(weight_part, ('row', 'col'))]
    reduce_scatter x1 -> x0, waiting for transfers between devices: 66.2 us -> none  [on_device(): lax.psum_scatter(placed.reshape(pieces * node_count, feat_width), 'col',...]
    pallas_call x0 -> x1, Pallas kernels: none -> 59.1 us  [on_device(): pl.pallas_call(kernel, out_shape=(jax.ShapeDtypeStruct((nodes, width), BF...]
    dot_general x15 -> x0, matrix products: 41.4 us -> none  [the longest x1 7.03 us: on_device(): jnp.einsum('apb,apif->abif', sub_cols.astype(jnp.float32), product, preci...]
    all_to_all x2 -> x0, waiting for transfers between devices: 31.2 us -> none  [the longest x1 18.3 us: on_device(): lax.all_to_all(remote_back, 'row', split_axis=0, concat_axis=0, tiled=True)]
    dot_general x6 -> x0, local copies, waits for them, and re-layouts: 21.9 us -> none  [the longest x1 5.55 us: on_device(): jnp.einsum('apik,apkf->apif', sub_tiles, picked, preferred_element_type=j...]
    all_to_all x2 -> x0, starting transfers between devices: 10.4 us -> none  [the longest x1 5.99 us: on_device(): lax.all_to_all(outgoing, 'row', split_axis=0, concat_axis=0, tiled=True)]
    unnamed x17 -> x24, local copies, waits for them, and re-layouts: 2.43 us -> 12.4 us
  transfers between devices with their start and end apart: 5 -> 0, of which waited for: 4 -> 0; matrix products, arithmetic and copies ran while one was open for 19% -> 0% of each run, Pallas kernels for 0% -> 0%
where the time goes in v1:
time: 72.9 us; the launch traced here: 72.2 us
  Pallas kernels  59.1 us (81%)
  local copies, waits for them, and re-layouts  12.4 us (17%)
    pallas_call x1, Pallas kernels, on_device(): pl.pallas_call(kernel, out_shape=(jax.ShapeDtypeStruct((nodes, width), BF...  59.1 us
    unnamed x24, local copies, waits for them, and re-layouts  12.4 us

profile of v1, /device:TPU:1, one launch (start us, length us, event | category | flops | bytes accessed | tf_op | source)
XLA Modules:
  0.0 72.2 jit_solution(1733507722507978130)
XLA Ops:
  0.6 0.8 %copy.15.send_index = s32[8,4]{1,0:T(8,128)S(1)} copy(s32[8,4]{0,1:T(4,128)} %param.20) | data formatting | bytes 256 | tf_op args[8]
  1.4 0.8 %copy.16.remote_rows = s32[8,4]{1,0:T(8,128)S(1)} copy(s32[8,4]{0,1:T(4,128)} %param.22) | data formatting | bytes 256 | tf_op args[10]
  2.1 0.8 %copy.17.remote_live = s32[8,4]{1,0:T(8,128)S(1)} copy(s32[8,4]{0,1:T(4,128)} %param.23) | data formatting | bytes 256 | tf_op args[11]
  2.9 0.0 copy-start
  2.9 1.6 %copy-done = bf16[64,128,128]{2,1,0:T(8,128)(2,1)S(1)} copy-done((bf16[64,128,128]{2,1,0:T(8,128)(2,1)S(1)}, bf16[64,128,128]{2,1,0:T(8,128)(2,1)}, u32[]{:S(2)}) %copy-start) | copy-done | bytes 2097176
  4.5 0.0 copy-start.1
  4.5 1.2 %copy-done.1 = bf16[32,128,128]{2,1,0:T(8,128)(2,1)S(1)} copy-done((bf16[32,128,128]{2,1,0:T(8,128)(2,1)S(1)}, bf16[32,128,128]{2,1,0:T(8,128)(2,1)}, u32[]{:S(2)}) %copy-start.1) | copy-done | bytes 1048600
  5.7 0.0 copy-start.2
  5.7 0.9 %copy-done.2 = bf16[1024,128]{1,0:T(8,128)(2,1)S(1)} copy-done((bf16[1024,128]{1,0:T(8,128)(2,1)S(1)}, bf16[1024,128]{1,0:T(8,128)(2,1)}, u32[]{:S(2)}) %copy-start.2) | copy-done | bytes 262168
  6.7 0.0 copy-start.3
  6.7 0.9 %copy-done.3 = bf16[1024,128]{1,0:T(8,128)(2,1)S(1)} copy-done((bf16[1024,128]{1,0:T(8,128)(2,1)S(1)}, bf16[1024,128]{1,0:T(8,128)(2,1)}, u32[]{:S(2)}) %copy-start.3) | copy-done | bytes 262168
  7.6 0.0 copy-start.4
  7.6 0.8 %copy-done.4 = bf16[128,128]{1,0:T(8,128)(2,1)S(1)} copy-done((bf16[128,128]{1,0:T(8,128)(2,1)S(1)}, bf16[128,128]{1,0:T(8,128)(2,1)}, u32[]{:S(2)}) %copy-start.4) | copy-done | bytes 32792
  8.4 0.7 copy-done.5
  9.1 0.0 copy-start.6
  9.1 0.7 copy-done.6
  9.7 0.0 copy-start.7
  9.7 0.7 copy-done.7
  10.4 0.0 copy-start.8
  10.4 0.7 copy-done.8
  11.0 59.1 %shard_map.139 = (bf16[1024,128]{1,0:T(8,128)(2,1)S(1)}, bf16[1024,128]{1,0:T(8,128)(2,1)S(1)}, f32[128,128]{1,0:T(8,128)S(1)}) custom-call(bf16[1024,128]{1,0:T(8,128)(2,1)S(1)} %copy-done.2, bf16[128,128]{1,0:T(8,128)(2,1)S(1)} %copy-done.4, bf16[1024,128]{1,0:T(8,128)(2,1)S(1)} %copy-done.3, s32[8,128]{1,0:T(8,128)S(1)} %bitcast.1, s32[64]{0:T(128)S(1)} %copy-done.6, ...), custom_call_target="tpu_custom_call" | custom-call | tf_op jit(solution)/shard_map/pallas_call | solution.py:496
  70.2 0.7 copy.21
  70.9 0.7 copy.22
  71.6 0.6 copy.23
  (1 shorter events, 0.0 us)
Async XLA Ops:
  2.9 1.6 %copy-start = (bf16[64,128,128]{2,1,0:T(8,128)(2,1)S(1)}, bf16[64,128,128]{2,1,0:T(8,128)(2,1)}, u32[]{:S(2)}) copy-start(bf16[64,128,128]{2,1,0:T(8,128)(2,1)} %tile_hbm.1) | copy-start | bytes 6291460
  4.5 1.2 %copy-start.1 = (bf16[32,128,128]{2,1,0:T(8,128)(2,1)S(1)}, bf16[32,128,128]{2,1,0:T(8,128)(2,1)}, u32[]{:S(2)}) copy-start(bf16[32,128,128]{2,1,0:T(8,128)(2,1)} %remote_hbm.1) | copy-start | bytes 3145732
  5.7 0.9 %copy-start.2 = (bf16[1024,128]{1,0:T(8,128)(2,1)S(1)}, bf16[1024,128]{1,0:T(8,128)(2,1)}, u32[]{:S(2)}) copy-start(bf16[1024,128]{1,0:T(8,128)(2,1)} %features.1) | copy-start | bytes 786436
  6.7 0.9 %copy-start.3 = (bf16[1024,128]{1,0:T(8,128)(2,1)S(1)}, bf16[1024,128]{1,0:T(8,128)(2,1)}, u32[]{:S(2)}) copy-start(bf16[1024,128]{1,0:T(8,128)(2,1)} %cotangent.1) | copy-start | bytes 786436
  7.6 0.8 %copy-start.4 = (bf16[128,128]{1,0:T(8,128)(2,1)S(1)}, bf16[128,128]{1,0:T(8,128)(2,1)}, u32[]{:S(2)}) copy-start(bf16[128,128]{1,0:T(8,128)(2,1)} %weight.1) | copy-start | bytes 98308
  8.4 0.7 copy-start.5
  9.1 0.7 copy-start.6
  9.7 0.7 copy-start.7
  10.4 0.7 copy-start.8
